TPU v7x, 32 devices: a whole 2x2x4 slice. The times are simulated.
32 devices in a mesh: groups: 2 (over x), dp: 16 (over z, y, core).
Axes of the slice: x: 2, y: 2, z: 4, core: 2. Of those that a mesh axis runs over, the one named last changes fastest.
Arguments:
- queries: bfloat16 [256, 4096], P(('groups', 'dp')), parts along dimension 0, may hold values from -0.4 to 0.4
- passages: bfloat16 [256, 4096], P(('groups', 'dp')), parts along dimension 0, may hold values from -0.6 to 0.6
- negatives: bfloat16 [8192, 4096], P(('groups', 'dp')), parts along dimension 0, may hold values from -0.5 to 0.5
- pairs: int32 [3584, 2], P(('groups', 'dp')), parts along dimension 0, may hold values from 0 to 4095, as said below
Outputs:
- losses: float32 [256], P(('groups', 'dp')), parts along dimension 0
- grad_queries: float32 [256, 4096], P(('groups', 'dp')), parts along dimension 0
- grad_passages: float32 [256, 4096], P(('groups', 'dp')), parts along dimension 0
- grad_negatives: float32 [8192, 4096], P(('groups', 'dp')), parts along dimension 0
There are 2 independent parts, one for each index of `groups`. A program takes and returns all parts, laid end to end along the dimension named above; each array names one. Nothing has to cross between parts.
Inputs may be any that keep to these rules, and one draw needn't show every extreme that they name: Column 0 is a query of the device holding the pair, below 8; column 1 is a row of negatives. Queries have varying numbers of pairs. Among the 112 pairs of one device at most 7 name rows held by any one device, and in every draw one device holds rows named by exactly 7 pairs of every device.
All inputs are finite; a program needn't handle non-finite values.
Results may differ from a plain program's by a relative error of at most 0.0081.
Values may be sent and summed in bfloat16 or wider, within the bound.
A program may use at most 128 MiB of HBM per device.

v0:
```python
import jax
import jax.numpy as jnp
from jax import lax
from jax.sharding import PartitionSpec as P

inv_temp = 50.0
norm_eps = 1e-06


def unit_rows(source_rows):
    raw_values = source_rows.astype(jnp.float32)
    row_scale = lax.rsqrt(jnp.sum(raw_values * raw_values, axis=1, keepdims=True) + norm_eps)
    return (raw_values, row_scale, (raw_values * row_scale).astype(jnp.bfloat16))


def norm_grad(raw_values, row_scale, upstream):
    dot_sum = jnp.sum(raw_values * upstream, axis=1, keepdims=True)
    return row_scale * upstream - row_scale * row_scale * row_scale * dot_sum * raw_values


def row_products(left_rows, right_rows):
    return lax.dot_general(
        left_rows, right_rows, (((1,), (1,)), ((), ())), preferred_element_type=jnp.float32
    )


def column_products(left_rows, right_rows):
    return lax.dot_general(
        left_rows, right_rows, (((0,), (0,)), ((), ())), preferred_element_type=jnp.float32
    )


def local(queries, passages, negatives, pairs):
    query_vals, query_scale, query_unit = unit_rows(queries)
    passage_vals, passage_scale, passage_unit = unit_rows(passages)
    negative_vals, negative_scale, negative_unit = unit_rows(negatives)
    device_count = lax.axis_size("dp")
    position = lax.axis_index("dp")
    query_count = queries.shape[0]
    width = queries.shape[1]
    pool_rows = negatives.shape[0]
    pair_count = pairs.shape[0]
    slot_count = max(2, (pair_count + device_count - 1) // device_count)
    query_of = pairs[:, 0]
    target = pairs[:, 1]
    owner_dev = target // pool_rows
    local_row = target - owner_dev * pool_rows
    pair_index = jnp.arange(pair_count)
    earlier_same = (owner_dev[None, :] == owner_dev[:, None]) & (
        pair_index[None, :] < pair_index[:, None]
    )
    slot_rank = jnp.sum(earlier_same.astype(jnp.int32), axis=1)
    flat_slot = owner_dev * slot_count + slot_rank
    wanted = jnp.full((device_count * slot_count,), -1, jnp.int32).at[flat_slot].set(local_row)
    wanted = wanted.reshape(device_count, slot_count)
    asking = jnp.take(query_unit, query_of, axis=0)
    slot_queries = (
        jnp.zeros((device_count * slot_count, width), jnp.bfloat16).at[flat_slot].set(asking)
    )
    slot_queries = slot_queries.reshape(device_count, slot_count, width)
    asked_rows = lax.all_to_all(wanted, "dp", split_axis=0, concat_axis=0, tiled=True)
    valid = asked_rows >= 0
    picked = jnp.take(negative_unit, jnp.maximum(asked_rows, 0), axis=0)
    picked = jnp.where(valid[:, :, None], picked, jnp.zeros_like(picked))
    returned = lax.all_to_all(picked, "dp", split_axis=0, concat_axis=0, tiled=True)
    fetched, asked_rows = (returned, asked_rows)
    all_passages = lax.all_gather(passage_unit, "dp", axis=0, tiled=True)
    scores = inv_temp * row_products(query_unit, all_passages)
    hard_rows = jnp.take(fetched.reshape(device_count * slot_count, width), flat_slot, axis=0)
    owned_by = jnp.arange(query_count)[:, None] == query_of[None, :]
    hard_all = row_products(query_unit, hard_rows)
    hard_score = inv_temp * jnp.sum(jnp.where(owned_by, hard_all, 0.0), axis=0)
    hard_sums = jnp.sum(jnp.where(owned_by, jnp.exp(hard_score)[None, :], 0.0), axis=1)
    log_total = jnp.log(jnp.sum(jnp.exp(scores), axis=1) + hard_sums)
    positive = position * query_count + jnp.arange(query_count)
    is_positive = jnp.arange(all_passages.shape[0])[None, :] == positive[:, None]
    losses = log_total - jnp.sum(jnp.where(is_positive, scores, 0.0), axis=1)
    weight = (jnp.exp(scores - log_total[:, None]) - is_positive.astype(jnp.float32)).astype(
        jnp.bfloat16
    )
    hard_weight = jnp.exp(hard_score - jnp.take(log_total, query_of)).astype(jnp.bfloat16)
    hard_matrix = jnp.where(owned_by, hard_weight[None, :], jnp.zeros((), jnp.bfloat16))
    query_grad = inv_temp * (
        jnp.dot(weight, all_passages, preferred_element_type=jnp.float32)
        + jnp.dot(hard_matrix, hard_rows, preferred_element_type=jnp.float32)
    )
    grad_queries = norm_grad(query_vals, query_scale, query_grad)
    every_total = lax.all_gather(log_total, "dp", axis=0, tiled=True)
    row_piece = lax.all_gather(query_unit, "dp", axis=0, tiled=True)
    row_total = row_piece.shape[0]
    piece_scores = inv_temp * row_products(row_piece, passage_unit)
    row_ids = jnp.arange(row_total)
    matching = row_ids[:, None] == positive[None, :]
    piece_weight = (
        jnp.exp(piece_scores - every_total[:, None]) - matching.astype(jnp.float32)
    ).astype(jnp.bfloat16)
    passage_grad = inv_temp * column_products(piece_weight, row_piece)
    grad_passages = norm_grad(passage_vals, passage_scale, passage_grad)
    slot_weight = (
        jnp.zeros((device_count * slot_count,), jnp.bfloat16).at[flat_slot].set(hard_weight)
    )
    slot_weight = slot_weight.reshape(device_count, slot_count)
    got_rows, got_weight = (
        lax.all_to_all(slot_queries, "dp", split_axis=0, concat_axis=0, tiled=True),
        lax.all_to_all(slot_weight, "dp", split_axis=0, concat_axis=0, tiled=True),
    )
    placing = jnp.arange(pool_rows)[:, None] == asked_rows.reshape(-1)[None, :]
    spread = jnp.where(placing, got_weight.reshape(-1)[None, :], jnp.zeros((), jnp.bfloat16))
    pool_grad = inv_temp * jnp.dot(
        spread, got_rows.reshape(-1, width), preferred_element_type=jnp.float32
    )
    grad_negatives = norm_grad(negative_vals, negative_scale, pool_grad)
    return (losses, grad_queries, grad_passages, grad_negatives)


def solution(mesh):
    placed = (
        P(("groups", "dp"), None),
        P(("groups", "dp"), None),
        P(("groups", "dp"), None),
        P(("groups", "dp"), None),
    )
    return jax.shard_map(
        local,
        mesh=mesh,
        in_specs=placed,
        out_specs=(
            P(("groups", "dp")),
            P(("groups", "dp"), None),
            P(("groups", "dp"), None),
            P(("groups", "dp"), None),
        ),
        check_vma=False,
    )
```

profile of v0, /device:TPU:0, one launch (start us, length us, event | category | flops | bytes accessed | tf_op | source)
XLA Modules:
  0.0 172.2 jit_solution(2180094502477425180)
XLA Ops:
  10.4 7.4 %all-to-all-start = ((s32[16,1,7]{2,1,0:T(1,128)}), s32[16,1,7]{2,1,0:T(1,128)S(1)}, u32[]{:S(2)}, u32[]{:S(2)}) async-start(s32[16,1,7]{2,1,0:T(1,128)} %bitcast.6), calls=%async_computation | async-start | bytes 16384 | tf_op jit(solution)/shard_map/all_to_all | solution.py:61
  18.9 1.6 fusion.20
  22.1 2.1 %fusion = f32[256]{0:T(256)S(1)} fusion(bf16[256,4096]{1,0:T(8,128)(2,1)} %param.6), kind=kLoop, calls=%fused_computation.11 | loop fusion | flops 3145472 | bytes 2098176 | tf_op jit(solution)/shard_map/reduce_sum | solution.py:12
  25.2 4.8 %scatter_custom_fusion.2 = bf16[112,4096]{1,0:T(8,128)(2,1)S(1)} fusion(s32[112]{0:T(128)S(1)} %bitcast.55, pred[112]{0:T(512)(128)(4,1)S(1)} %and_bitcast_fusion, bf16[]{:T(256)} %constant.68.clone.1, bf16[]{:T(256)} %constant.67.clone.1, bf16[8,4096]{1,0:T(8,128)(2,1)S(1)} %fusion.16, s32[1024]{0:T(1024)S(1)} %pad_clamp_fusion), kind=kCustom, calls=%fused_computation.25 | custom fusion | flops 458752 | bytes 987652 | tf_op jit(solution)/shard_map/scatter | solution.py:58
  30.0 1.3 reshape.177
  31.3 6.1 %all-to-all-start.3 = ((bf16[16,7,4096]{2,1,0:T(8,128)(2,1)}), bf16[16,7,4096]{2,1,0:T(8,128)(2,1)}, u32[]{:S(2)}, u32[]{:S(2)}) async-start(bf16[16,7,4096]{2,1,0:T(8,128)(2,1)} %reshape.177), calls=%async_computation.3 | async-start | bytes 2097152 | tf_op jit(solution)/shard_map/all_to_all | solution.py:104
  37.4 2.2 %fusion.1 = bf16[256,4096]{1,0:T(8,128)(2,1)S(1)} fusion(bf16[256,4096]{1,0:T(8,128)(2,1)} %param.6, f32[256]{0:T(256)S(1)} %add_rsqrt_fusion), kind=kLoop, calls=%fused_computation.12 | loop fusion | flops 3145728 | bytes 4195328 | tf_op jit(solution)/shard_map/convert_element_type | solution.py:13
  41.5 1.2 select_select_fusion
  42.7 21.3 %all-to-all-done.3 = bf16[16,7,4096]{2,1,0:T(8,128)(2,1)} async-done(((bf16[16,7,4096]{2,1,0:T(8,128)(2,1)}), bf16[16,7,4096]{2,1,0:T(8,128)(2,1)}, u32[]{:S(2)}, u32[]{:S(2)}) %all-to-all-start.3) | async-done | bytes 917536 | tf_op jit(solution)/shard_map/all_to_all | solution.py:104
  64.0 7.8 %all-to-all-start.1 = ((bf16[16,7,4096]{2,1,0:T(8,128)(2,1)}), bf16[16,7,4096]{2,1,0:T(8,128)(2,1)S(1)}, u32[]{:S(2)}, u32[]{:S(2)}) async-start(bf16[16,7,4096]{2,1,0:T(8,128)(2,1)} %select_select_fusion), calls=%async_computation.1 | async-start | bytes 2097152 | tf_op jit(solution)/shard_map/all_to_all | solution.py:65
  75.0 1.5 reshape.178
  76.5 19.4 %all-to-all-done.1 = bf16[16,7,4096]{2,1,0:T(8,128)(2,1)S(1)} async-done(((bf16[16,7,4096]{2,1,0:T(8,128)(2,1)}), bf16[16,7,4096]{2,1,0:T(8,128)(2,1)S(1)}, u32[]{:S(2)}, u32[]{:S(2)}) %all-to-all-start.1) | async-done | bytes 917536 | tf_op jit(solution)/shard_map/all_to_all | solution.py:65
  96.2 2.0 %gather_fusion.1 = bf16[112,4096]{1,0:T(8,128)(2,1)} fusion(bf16[112,4096]{1,0:T(8,128)(2,1)S(1)} %reshape.176, s32[1024]{0:T(1024)S(1)} %pad_clamp_fusion.1), kind=kCustom, calls=%fused_computation.1 | custom fusion | bytes 1835456 | tf_op jit(solution)/shard_map/jit(_take)/gather | solution.py:69
  98.3 1.8 %fusion.8 = f32[112]{0:T(128)S(1)} fusion(bf16[8,4096]{1,0:T(8,128)(2,1)S(1)} %copy-done.2, bf16[112,4096]{1,0:T(8,128)(2,1)} %gather_fusion.1, pred[112]{0:T(512)(128)(4,1)S(1)} %get-tuple-element.8, s32[112]{0:T(128)S(1)} %get-tuple-element.18), kind=kOutput, calls=%fused_computation.22 | convolution fusion | flops 7801360 | bytes 984048 | tf_op jit(solution)/shard_map/dot_general | solution.py:22
  100.2 1.8 %select_reduce_fusion = (f32[8]{0:T(128)S(1)}, f32[8]{0:T(128)S(1)}, f32[8,128]{1,0:T(8,128)S(1)}) fusion(s32[8]{0:T(128)S(1)} %iota_add_fusion, bf16[8,4096]{1,0:T(8,128)(2,1)S(1)} %copy-done.2, bf16[128,4096]{1,0:T(8,128)(2,1)} %all-gather.3.cloned.1.call-done), kind=kOutput, calls=%fused_computation.62 | convolution fusion | flops 8393712 | bytes 1118304 | tf_op jit(solution)/shard_map/dot_general | solution.py:22
  102.1 36.0 %all-reduce = f32[128]{0:T(128)S(1)} all-reduce(f32[128]{0:T(128)S(1)} %get-tuple-element.6), channel_id=1, replica_groups=mesh['groups'=2,'dp'=16] {'dp'}, use_global_device_ids=true, to_apply=%add | all-reduce | flops 128 | bytes 1024
  138.1 2.6 %fusion.21 = (f32[8]{0:T(128)S(1)}, f32[8,4096]{1,0:T(8,128)S(1)}) fusion(bf16[8,4096]{1,0:T(8,128)(2,1)S(1)} %copy-done.3, bf16[128,4096]{1,0:T(8,128)(2,1)} %all-gather.5.cloned.1.call-done, s32[8]{0:T(128)S(1)} %iota_add_fusion, f32[128]{0:T(128)S(1)} %all-reduce, f32[8]{0:T(128)S(1)} %add_rsqrt_fusion.1), kind=kOutput, calls=%fused_computation.45 | convolution fusion | flops 17012728 | bytes 1245792 | tf_op jit(solution)/shard_map/dot_general | solution.py:28
  141.4 5.0 %exponential_convert_fusion = bf16[112]{0:T(256)(128)(2,1)S(1)} fusion(f32[112]{0:T(128)S(1)} %fusion.8, f32[]{:T(128)} %bitcast.11, f32[]{:T(128)} %bitcast.12, f32[]{:T(128)} %bitcast.13, f32[]{:T(128)} %bitcast.14, f32[]{:T(128)} %bitcast.15, f32[]{:T(128)} %bitcast.16, f32[]{:T(128)} %bitcast.17, f32[]{:T(128)} %bitcast.18, s32[112,2]{0,1:T(2,128)S(1)} %copy-done.5), kind=kLoop, calls=%fused_computation.112 | loop fusion | flops 2688 | bytes 1152 | tf_op jit(solution)/shard_map/convert_element_type | solution.py:81
  146.4 1.2 scatter_custom_fusion.1
  147.7 1.5 fusion.33
  149.2 1.6 fusion.17
  151.6 3.5 %all-to-all-start.2 = ((bf16[16,1,7]{2,1,0:T(2,128)(2,1)}), bf16[16,1,7]{2,1,0:T(2,128)(2,1)S(1)}, u32[]{:S(2)}, u32[]{:S(2)}) async-start(bf16[16,1,7]{2,1,0:T(2,128)(2,1)} %all_to_all.24), calls=%async_computation.2 | async-start | bytes 16384 | tf_op jit(solution)/shard_map/all_to_all | solution.py:105
  157.0 4.3 %all-to-all-done.2 = bf16[16,1,7]{2,1,0:T(2,128)(2,1)S(1)} async-done(((bf16[16,1,7]{2,1,0:T(2,128)(2,1)}), bf16[16,1,7]{2,1,0:T(2,128)(2,1)S(1)}, u32[]{:S(2)}, u32[]{:S(2)}) %all-to-all-start.2) | async-done | bytes 256 | tf_op jit(solution)/shard_map/all_to_all | solution.py:105
  162.4 3.0 %fusion.3 = f32[256,4096]{1,0:T(8,128)} fusion(bf16[256,4096]{1,0:T(8,128)(2,1)S(1)} %copy-done, f32[256,4096]{1,0:T(8,128)S(1)} %get-tuple-element.37, f32[256]{0:T(256)S(1)} %get-tuple-element.15, f32[256]{0:T(256)S(1)} %get-tuple-element.14), kind=kLoop, calls=%fused_computation.14 | loop fusion | flops 4194304 | bytes 10487808 | tf_op jit(solution)/shard_map/sub | solution.py:18
  (67 shorter events, 16.3 us)
Async XLA Ops:
  10.4 20.9 %all-to-all-start = ((s32[16,1,7]{2,1,0:T(1,128)}), s32[16,1,7]{2,1,0:T(1,128)S(1)}, u32[]{:S(2)}, u32[]{:S(2)}) async-start(s32[16,1,7]{2,1,0:T(1,128)} %bitcast.6), calls=%async_computation | async-start | bytes 16384 | tf_op jit(solution)/shard_map/all_to_all | solution.py:61
  17.8 82.4 %all-gather.3.cloned.1.call-start = ((), (), s32[]{:S(2)}) async-start(), calls=%async_computation.4 | async-start | bytes 1114112 | tf_op jit(solution)/shard_map/all_gather | solution.py:67
  25.2 14.4 %copy-start.1 = (bf16[8,4096]{1,0:T(8,128)(2,1)}, bf16[8,4096]{1,0:T(8,128)(2,1)S(1)}, u32[]{:S(2)}) copy-start(bf16[8,4096]{1,0:T(8,128)(2,1)S(1)} %fusion.16) | copy-start | bytes 196612
  31.3 32.7 %all-to-all-start.3 = ((bf16[16,7,4096]{2,1,0:T(8,128)(2,1)}), bf16[16,7,4096]{2,1,0:T(8,128)(2,1)}, u32[]{:S(2)}, u32[]{:S(2)}) async-start(bf16[16,7,4096]{2,1,0:T(8,128)(2,1)} %reshape.177), calls=%async_computation.3 | async-start | bytes 2097152 | tf_op jit(solution)/shard_map/all_to_all | solution.py:104
  41.2 31.4 %copy-start.6 = (u32[32]{0:T(128)S(1)}, u32[32]{0:T(128)}, u32[]{:S(2)}) copy-start(u32[32]{0:T(128)} %constant.113) | copy-start | bytes 388
  64.0 31.9 %all-to-all-start.1 = ((bf16[16,7,4096]{2,1,0:T(8,128)(2,1)}), bf16[16,7,4096]{2,1,0:T(8,128)(2,1)S(1)}, u32[]{:S(2)}, u32[]{:S(2)}) async-start(bf16[16,7,4096]{2,1,0:T(8,128)(2,1)} %select_select_fusion), calls=%async_computation.1 | async-start | bytes 2097152 | tf_op jit(solution)/shard_map/all_to_all | solution.py:65
  71.8 66.3 %all-gather.5.cloned.1.call-start = ((), (), s32[]{:S(2)}) async-start(), calls=%async_computation.5 | async-start | bytes 1114112 | tf_op jit(solution)/shard_map/all_gather | solution.py:89
  96.2 2.1 %copy-start.2 = (bf16[8,4096]{1,0:T(8,128)(2,1)S(1)}, bf16[8,4096]{1,0:T(8,128)(2,1)}, u32[]{:S(2)}) copy-start(bf16[8,4096]{1,0:T(8,128)(2,1)} %copy-done.1) | copy-start | bytes 196612
  96.2 41.9 %copy-start.3 = (bf16[8,4096]{1,0:T(8,128)(2,1)S(1)}, bf16[8,4096]{1,0:T(8,128)(2,1)}, u32[]{:S(2)}) copy-start(bf16[8,4096]{1,0:T(8,128)(2,1)} %param.5) | copy-start | bytes 196612
  98.3 43.1 %copy-start.5 = (s32[112,2]{0,1:T(2,128)S(1)}, s32[112,2]{0,1:T(2,128)}, u32[]{:S(2)}) copy-start(s32[112,2]{0,1:T(2,128)} %param.7) | copy-start | bytes 2692
  98.3 50.9 %copy-start.4 = (bf16[8,4096]{1,0:T(8,128)(2,1)S(1)}, bf16[8,4096]{1,0:T(8,128)(2,1)}, u32[]{:S(2)}) copy-start(bf16[8,4096]{1,0:T(8,128)(2,1)} %param.4) | copy-start | bytes 196612
  98.3 63.2 %copy-start = (bf16[256,4096]{1,0:T(8,128)(2,1)S(1)}, bf16[256,4096]{1,0:T(8,128)(2,1)}, u32[]{:S(2)}) copy-start(bf16[256,4096]{1,0:T(8,128)(2,1)} %param.6) | copy-start | bytes 6291460
  151.6 9.8 %all-to-all-start.2 = ((bf16[16,1,7]{2,1,0:T(2,128)(2,1)}), bf16[16,1,7]{2,1,0:T(2,128)(2,1)S(1)}, u32[]{:S(2)}, u32[]{:S(2)}) async-start(bf16[16,1,7]{2,1,0:T(2,128)(2,1)} %all_to_all.24), calls=%async_computation.2 | async-start | bytes 16384 | tf_op jit(solution)/shard_map/all_to_all | solution.py:105
Sparse Core Ops, SparseCore 0:
  21.4 45.9 all-gather.2
  75.4 43.4 all-gather.4
where the time goes:
time: 173 us; the launch traced here: 172 us
  waiting for transfers between devices  45.7 us (26%)
  blocking collectives  36 us (21%)
  other arithmetic  28 us (16%)
  starting transfers between devices  24.8 us (14%)
  between operations  15 us (9%)
  local copies, waits for them, and re-layouts  12.6 us (7%)
  matrix products  10.1 us (6%)
    unnamed x1, blocking collectives  36 us
    all_to_all x1, waiting for transfers between devices, local(): lax.all_to_all(slot_queries, 'dp', split_axis=0, concat_axis=0, tiled=True)  21.3 us
    all_to_all x1, waiting for transfers between devices, local(): lax.all_to_all(picked, 'dp', split_axis=0, concat_axis=0, tiled=True)  19.4 us
    all_to_all x1, starting transfers between devices, local(): lax.all_to_all(picked, 'dp', split_axis=0, concat_axis=0, tiled=True)  7.83 us
    all_to_all x1, starting transfers between devices, local(): lax.all_to_all(wanted, 'dp', split_axis=0, concat_axis=0, tiled=True)  7.39 us
    all_to_all x1, starting transfers between devices, local(): lax.all_to_all(slot_queries, 'dp', split_axis=0, concat_axis=0, tiled=True)  6.06 us
    convert_element_type x1, other arithmetic, local(): jnp.exp(hard_score - jnp.take(log_total, query_of)).astype(jnp.bfloat16)  5.03 us
    scatter x1, other arithmetic, local(): jnp.zeros((device_count * slot_count, width), jnp.bfloat16).at[flat_slot]  4.82 us
  transfers between devices with their start and end apart: 6, of which 3 were waited for; matrix products, arithmetic and copies ran while one was open for 17% of the time, Pallas kernels for 0%

commit v1 on v0

v1 whole, which is shorter than its diff:
```python
import functools

import jax
import jax.numpy as jnp
from jax import lax
from jax.experimental import pallas as pl
from jax.experimental.pallas import tpu as pltpu
from jax.sharding import PartitionSpec as P

inv_temp = 50.0
norm_eps = 1e-06
f32 = jnp.float32
bf16 = jnp.bfloat16
EXTRA = 128


def dot_nt(a, b):
    return lax.dot_general(a, b, (((1,), (1,)), ((), ())), preferred_element_type=f32)


def dot_nn(a, b):
    return lax.dot_general(a, b, (((1,), (0,)), ((), ())), preferred_element_type=f32)


def norm_grad(raw, scale, up):
    dot_sum = jnp.sum(raw * up, axis=1, keepdims=True)
    return scale * up - scale * scale * scale * dot_sum * raw


def kernel(
    n, q_ref, p_ref, neg_ref, pairs_ref,
    loss_ref, gq_ref, gp_ref, gn_ref,
    qbuf, qfull, nraw, unit, nscale, counts, scores, expt, weights, ubuf, sibrecv, crecv, gnbuf,
    zsend, zsib, zbuf, acc,
    nsem, gsem, qs, qr, fs, fr, us, ur, cs, cr, zs, zr, zxs, zxr,
):
    qd, width = q_ref.shape
    half = width // 2
    pool = neg_ref.shape[0]
    npairs = pairs_ref.shape[0]
    nq = n * qd
    nc = n // 2
    me = lax.axis_index("dp")
    chip = me // 2
    core = me - 2 * chip
    sib = me + 1 - 2 * core

    def ahead(k):
        return lax.rem(chip + k, nc)

    def behind(k):
        return lax.rem(chip + nc - k, nc)

    def remote(src, dst, ssem, rsem, target):
        return pltpu.make_async_remote_copy(
            src_ref=src, dst_ref=dst, send_sem=ssem, recv_sem=rsem,
            device_id={"dp": target}, device_id_type=pl.DeviceIdType.MESH,
        )

    load = pltpu.make_async_copy(neg_ref, nraw, nsem)
    load.start()
    barrier = pltpu.get_barrier_semaphore()
    pl.semaphore_signal(barrier, inc=1, device_id={"dp": sib}, device_id_type=pl.DeviceIdType.MESH)

    @pl.loop(1, nc)
    def _(k):
        pl.semaphore_signal(
            barrier, inc=1, device_id={"dp": 2 * ahead(k) + core},
            device_id_type=pl.DeviceIdType.MESH,
        )

    qx = q_ref[...].astype(f32)
    qscale = lax.rsqrt(jnp.sum(qx * qx, axis=1, keepdims=True) + norm_eps)
    qu = qx * qscale
    qbuf[me, :, :half] = jnp.concatenate([qu[:, :half], qu[:, half:]], axis=0).astype(bf16)
    pv = pairs_ref[...].astype(f32)
    diag = lax.broadcasted_iota(jnp.int32, (npairs, EXTRA), 0) == lax.broadcasted_iota(
        jnp.int32, (npairs, EXTRA), 1
    )
    prow = jnp.sum(jnp.where(diag, pv[:, 0:1], 0.0), axis=0, keepdims=True)
    trow = jnp.sum(jnp.where(diag, pv[:, 1:2], 0.0), axis=0, keepdims=True)
    owner = jnp.floor((trow + 0.5) * (1.0 / pool))
    local_row = trow - owner * pool
    owner = jnp.where(lax.broadcasted_iota(jnp.int32, (1, EXTRA), 1) < npairs, owner, -1.0)
    rid = lax.broadcasted_iota(jnp.int32, (16, EXTRA), 0)
    meta = jnp.where(rid == 0, prow, jnp.where(rid == 1, owner, local_row))
    qbuf[me, :, half:] = meta.astype(bf16)

    pl.semaphore_wait(barrier, nc)

    def q_copy(k, target):
        return remote(qbuf.at[me], qbuf.at[me], qs.at[k], qr.at[k], target)

    @pl.loop(1, nc)
    def _(k):
        q_copy(k, 2 * ahead(k) + core).start()

    q_copy(0, sib).start()

    px = p_ref[...].astype(f32)
    pscale = lax.rsqrt(jnp.sum(px * px, axis=1, keepdims=True) + norm_eps)
    unit[pool : pool + 16, :] = jnp.concatenate(
        [px * pscale, jnp.zeros((16 - qd, width), f32)], axis=0
    ).astype(bf16)
    unit[pool + 16 :, :] = jnp.zeros((unit.shape[0] - pool - 16, width), bf16)
    load.wait()

    @pl.loop(0, pool // 16)
    def _(b):
        rows = pl.ds(pl.multiple_of(b * 16, 16), 16)
        x = nraw[rows, :].astype(f32)
        s = lax.rsqrt(jnp.sum(x * x, axis=1, keepdims=True) + norm_eps)
        nscale[rows, :] = s
        unit[rows, :] = (x * s).astype(bf16)

    def f_copy(k, c):
        slot = 2 * behind(k) + c
        return remote(qbuf.at[slot], qbuf.at[slot], fs.at[k], fr.at[k], sib)

    @pl.loop(1, nc)
    def _(k):
        slot = 2 * behind(k) + core
        remote(qbuf.at[slot], qbuf.at[slot], qs.at[k], qr.at[k], sib).wait_recv()
        f_copy(k, core).start()

    arow = lax.broadcasted_iota(jnp.int32, (unit.shape[0], nq), 0)
    counts[...] = jnp.where((arow >= pool) & (arow < pool + qd), 1.0, 0.0)
    mef = me.astype(f32)

    def place(j):
        a = qbuf[2 * j].astype(f32)
        b = qbuf[2 * j + 1].astype(f32)
        rows = pl.ds(pl.multiple_of(j * 16, 16), 16)
        qfull[rows, :half] = jnp.concatenate([a[:8, :half], b[:8, :half]], axis=0).astype(bf16)
        qfull[rows, half:] = jnp.concatenate([a[8:, :half], b[8:, :half]], axis=0).astype(bf16)
        pool_id = lax.broadcasted_iota(jnp.int32, (pool, EXTRA), 0).astype(f32)
        query_id = lax.broadcasted_iota(jnp.int32, (nq, EXTRA), 0).astype(f32)
        hot_t, hot_q = [], []
        for part, c in ((a, 0), (b, 1)):
            m = part[:8, half:]
            want = jnp.where(m[1:2] == mef, m[2:3], -1.0)
            ask = m[0:1] + ((2 * j + c) * qd).astype(f32)
            hot_t.append(jnp.where(pool_id == want, 1.0, 0.0).astype(bf16))
            hot_q.append(jnp.where(query_id == ask, 1.0, 0.0).astype(bf16))
        counts[:pool, :] += dot_nt(
            jnp.concatenate(hot_t, axis=1), jnp.concatenate(hot_q, axis=1)
        )

    remote(qbuf.at[sib], qbuf.at[sib], qs.at[0], qr.at[0], sib).wait_recv()
    place(chip)

    @pl.loop(1, nc)
    def _(k):
        f_copy(k, 1 - core).wait_recv()
        place(behind(k))

    zero = jnp.zeros((1, 128), f32)
    for m in range(nq // 128):
        cols = slice(m * 128, m * 128 + 128)
        s = inv_temp * dot_nt(unit[...], qfull[cols, :])
        scores[:, cols] = s
        e = counts[:, cols] * jnp.exp(s)
        zsend[:, cols] = jnp.broadcast_to(jnp.sum(e, axis=0, keepdims=True) + zero, (8, 128))
        expt[cols, :] = e.T.astype(bf16)

    z_sib = remote(zsend, zsib, zs.at[0], zr.at[0], sib)
    z_sib.start()

    step = 256

    @pl.loop(0, half // step)
    def _(b):
        left = pl.ds(pl.multiple_of(b * step, step), step)
        right = pl.ds(pl.multiple_of(half + b * step, step), step)
        for m in range(nq // 128):
            e = expt[m * 128 : m * 128 + 128, :]
            u0 = dot_nn(e, unit[:, left]).reshape(128 // 8, 8, step)
            u1 = dot_nn(e, unit[:, right]).reshape(128 // 8, 8, step)
            ubuf[m * 16 : m * 16 + 16, :, left] = jnp.concatenate([u0, u1], axis=1).astype(bf16)

    def u_copy(k, j):
        return remote(ubuf.at[2 * j + 1 - core], sibrecv.at[j], us.at[k], ur.at[k], sib)

    @pl.loop(1, nc + 1)
    def _(k):
        u_copy(lax.rem(k, nc), ahead(k)).start()

    z_sib.wait_recv()
    zbuf[chip] = zsend[...] + zsib[...]

    def z_copy(k, slot):
        return remote(zbuf.at[chip], zbuf.at[slot], zxs.at[k], zxr.at[k], 2 * ahead(k) + core)

    @pl.loop(1, nc)
    def _(k):
        z_copy(k, chip).start()

    def c_copy(k, j):
        return remote(
            ubuf.at[2 * j + core], crecv.at[k], cs.at[k], cr.at[k], 2 * j + core
        )

    @pl.loop(1, nc)
    def _(k):
        j = ahead(k)
        u_copy(k, j).wait_recv()
        ubuf[2 * j + core] = (
            ubuf[2 * j + core].astype(f32) + sibrecv[j].astype(f32)
        ).astype(bf16)
        c_copy(k, j).start()

    @pl.loop(1, nc)
    def _(k):
        z_copy(k, behind(k)).wait_recv()

    total = zbuf[0]
    for j in range(1, nc):
        total = total + zbuf[j]
    log_total = jnp.log(total)
    lane_q = lax.broadcasted_iota(jnp.int32, (8, nq), 1)
    row_q = lax.broadcasted_iota(jnp.int32, (8, nq), 0)
    own = lane_q == row_q + me * qd
    log_own = jnp.sum(jnp.where(own, log_total, 0.0), axis=1, keepdims=True)
    self_score = jnp.sum(
        jnp.where(own, scores[pool : pool + 8, :], 0.0), axis=1, keepdims=True
    )
    loss_ref[...] = log_own - self_score
    positive = (arow >= pool) & (
        arow - pool + me * qd == lax.broadcasted_iota(jnp.int32, arow.shape, 1)
    ) & (arow < pool + qd)
    w = counts[...] * jnp.exp(scores[...] - log_total[0:1]) - jnp.where(positive, 1.0, 0.0)
    weights[...] = w.astype(bf16)
    udot = jnp.sum(
        weights[:pool, :].astype(f32) * scores[:pool, :], axis=1, keepdims=True
    )

    scale_col = nscale[...]
    back = udot * scale_col
    wide = 512

    @pl.loop(0, width // wide)
    def _(b):
        cols = pl.ds(pl.multiple_of(b * wide, wide), wide)
        g = inv_temp * dot_nn(weights[:pool, :], qfull[:, cols])
        gnbuf[:, cols] = (
            scale_col * (g - back * nraw[:, cols].astype(f32))
        ).astype(bf16)

    save = pltpu.make_async_copy(gnbuf, gn_ref, gsem)
    save.start()

    pg = inv_temp * dot_nn(weights[pool : pool + 16, :], qfull[...])
    gp_ref[...] = norm_grad(px, pscale, pg[:qd])

    own16 = jnp.concatenate([own.astype(f32), jnp.zeros((8, nq), f32)], axis=0).astype(bf16)
    own_w = dot_nt(own16, weights[...]).astype(bf16)
    own_g = dot_nn(own_w, unit[...])[:qd]

    u_copy(0, chip).wait_recv()
    acc[...] = sibrecv[chip].astype(f32)

    @pl.loop(1, nc)
    def _(k):
        c_copy(k, behind(k)).wait_recv()
        acc[...] += crecv[k].astype(f32)

    rest = jnp.concatenate([acc[:8, :], acc[8:, :]], axis=1)
    qg = inv_temp * (own_g + rest * jnp.exp(-log_own))
    gq_ref[...] = norm_grad(qx, qscale, qg)

    q_copy(0, sib).wait_send()
    z_sib.wait_send()
    u_copy(0, chip).wait_send()

    @pl.loop(1, nc)
    def _(k):
        q_copy(k, sib).wait_send()
        f_copy(k, core).wait_send()
        z_copy(k, chip).wait_send()
        u_copy(k, ahead(k)).wait_send()
        c_copy(k, ahead(k)).wait_send()

    save.wait()


def local(queries, passages, negatives, pairs):
    n = lax.axis_size("dp")
    nc = n // 2
    qd, width = queries.shape
    pool = negatives.shape[0]
    nq = n * qd
    half = width // 2
    rows = pool + 128
    vm = pl.BlockSpec(memory_space=pltpu.VMEM)
    anys = pl.BlockSpec(memory_space=pl.ANY)
    dma = pltpu.SemaphoreType.DMA
    loss, gq, gp, gn = pl.pallas_call(
        functools.partial(kernel, n),
        out_shape=(
            jax.ShapeDtypeStruct((qd, 1), f32),
            jax.ShapeDtypeStruct((qd, width), f32),
            jax.ShapeDtypeStruct((qd, width), f32),
            jax.ShapeDtypeStruct((pool, width), bf16),
        ),
        in_specs=[vm, vm, anys, vm],
        out_specs=(vm, vm, vm, anys),
        scratch_shapes=[
            pltpu.VMEM((n, 16, half + EXTRA), bf16),
            pltpu.VMEM((nq, width), bf16),
            pltpu.VMEM((pool, width), bf16),
            pltpu.VMEM((rows, width), bf16),
            pltpu.VMEM((pool, 1), f32),
            pltpu.VMEM((rows, nq), f32),
            pltpu.VMEM((rows, nq), f32),
            pltpu.VMEM((nq, rows), bf16),
            pltpu.VMEM((rows, nq), bf16),
            pltpu.VMEM((n, 16, half), bf16),
            pltpu.VMEM((nc, 16, half), bf16),
            pltpu.VMEM((nc, 16, half), bf16),
            pltpu.VMEM((pool, width), bf16),
            pltpu.VMEM((8, nq), f32),
            pltpu.VMEM((8, nq), f32),
            pltpu.VMEM((nc, 8, nq), f32),
            pltpu.VMEM((16, half), f32),
            dma, dma,
            dma((nc,)), dma((nc,)), dma((nc,)), dma((nc,)), dma((nc,)), dma((nc,)),
            dma((nc,)), dma((nc,)), dma((1,)), dma((1,)), dma((nc,)), dma((nc,)),
        ],
        compiler_params=pltpu.CompilerParams(
            collective_id=0, has_side_effects=True,
            vmem_limit_bytes=(56 if n > 32 else 40) * 1024 * 1024,
        ),
    )(queries, passages, negatives, pairs)
    return loss.reshape(qd), gq, gp, gn.astype(f32)


def solution(mesh):
    rows = P(("groups", "dp"), None)
    return jax.shard_map(
        local,
        mesh=mesh,
        in_specs=(rows, rows, rows, rows),
        out_specs=(P(("groups", "dp")), rows, rows, rows),
        check_vma=False,
    )
```

time: 173 us -> 45.5 us (0.26)
  the two profiles are of different devices: /device:TPU:0 before, /device:TPU:29 now
where the time goes in v1:
time: 45.5 us; the launch traced here: 45.3 us
  Pallas kernels  36.1 us (79%)
  local copies, waits for them, and re-layouts  5.36 us (12%)
  other arithmetic  3.13 us (7%)
  between operations  0.65 us (1%)
    pallas_call x1, Pallas kernels, local(): pl.pallas_call(functools.partial(kernel, n), out_shape=(jax.ShapeDtypeStr...  36.1 us
    unnamed x9, local copies, waits for them, and re-layouts  5.36 us
    convert_element_type x1, other arithmetic, local(): return (loss.reshape(qd), gq, gp, gn.astype(f32))  2.5 us

profile of v1, /device:TPU:29, one launch (start us, length us, event | category | flops | bytes accessed | tf_op | source)
XLA Modules:
  0.0 45.3 jit_solution(9703814776012027494)
XLA Ops:
  0.6 0.8 %copy.9.pairs_ref = s32[112,2]{1,0:T(8,128)S(1)} copy(s32[112,2]{0,1:T(2,128)} %param.7) | data formatting | bytes 1792 | tf_op args[3]
  1.4 0.0 copy-start
  1.4 1.6 %copy-done = bf16[256,4096]{1,0:T(8,128)(2,1)S(1)} copy-done((bf16[256,4096]{1,0:T(8,128)(2,1)S(1)}, bf16[256,4096]{1,0:T(8,128)(2,1)}, u32[]{:S(2)}) %copy-start) | copy-done | bytes 2097176
  3.0 0.0 copy-start.1
  3.0 0.8 %copy-done.1 = bf16[8,4096]{1,0:T(8,128)(2,1)S(1)} copy-done((bf16[8,4096]{1,0:T(8,128)(2,1)S(1)}, bf16[8,4096]{1,0:T(8,128)(2,1)}, u32[]{:S(2)}) %copy-start.1) | copy-done | bytes 65560
  3.8 0.0 copy-start.2
  3.8 0.8 %copy-done.2 = bf16[8,4096]{1,0:T(8,128)(2,1)S(1)} copy-done((bf16[8,4096]{1,0:T(8,128)(2,1)S(1)}, bf16[8,4096]{1,0:T(8,128)(2,1)}, u32[]{:S(2)}) %copy-start.2) | copy-done | bytes 65560
  4.7 36.1 %shard_map.75 = (f32[8,1]{1,0:T(8,128)S(1)}, f32[8,4096]{1,0:T(8,128)S(1)}, f32[8,4096]{1,0:T(8,128)S(1)}, bf16[256,4096]{1,0:T(8,128)(2,1)S(1)}) custom-call(bf16[8,4096]{1,0:T(8,128)(2,1)S(1)} %copy-done.1, bf16[8,4096]{1,0:T(8,128)(2,1)S(1)} %copy-done.2, bf16[256,4096]{1,0:T(8,128)(2,1)S(1)} %copy-done, s32[112,2]{1,0:T(8,128)S(1)} %copy.9.pairs_ref), custom_call_target="tpu_custom_call" | custom-call | tf_op jit(solution)/shard_map/pallas_call | solution.py:297
  40.8 0.6 %reduce = f32[8]{0:T(128)} reduce(f32[8,1]{1,0:T(8,128)S(1)} %get-tuple-element.8, f32[]{:T(128)} %constant.3), dimensions={1}, to_apply=%get-tuple-element.8.reduce_sub_computation | reduce | bytes 68 | tf_op jit(solution)/shard_map/pallas_call | solution.py:297
  41.5 2.5 %convert_element_type.3 = f32[256,4096]{1,0:T(8,128)} convert(bf16[256,4096]{1,0:T(8,128)(2,1)S(1)} %get-tuple-element.11) | non-fusion elementwise | flops 1048576 | bytes 6291456 | tf_op jit(solution)/shard_map/convert_element_type | solution.py:334
  44.0 0.7 %copy.12 = f32[8,4096]{1,0:T(8,128)} copy(f32[8,4096]{1,0:T(8,128)S(1)} %get-tuple-element.17) | data formatting | bytes 262144
  44.6 0.7 %copy.13 = f32[8,4096]{1,0:T(8,128)} copy(f32[8,4096]{1,0:T(8,128)S(1)} %get-tuple-element.18) | data formatting | bytes 262144
Async XLA Ops:
  1.4 1.6 %copy-start = (bf16[256,4096]{1,0:T(8,128)(2,1)S(1)}, bf16[256,4096]{1,0:T(8,128)(2,1)}, u32[]{:S(2)}) copy-start(bf16[256,4096]{1,0:T(8,128)(2,1)} %neg_ref.1) | copy-start | bytes 6291460
  3.0 0.8 %copy-start.1 = (bf16[8,4096]{1,0:T(8,128)(2,1)S(1)}, bf16[8,4096]{1,0:T(8,128)(2,1)}, u32[]{:S(2)}) copy-start(bf16[8,4096]{1,0:T(8,128)(2,1)} %q_ref.1) | copy-start | bytes 196612
  3.8 0.8 %copy-start.2 = (bf16[8,4096]{1,0:T(8,128)(2,1)S(1)}, bf16[8,4096]{1,0:T(8,128)(2,1)}, u32[]{:S(2)}) copy-start(bf16[8,4096]{1,0:T(8,128)(2,1)} %p_ref.1) | copy-start | bytes 196612

commit v2 on v1

--- a/solution.py
+++ b/solution.py
@@ -27,23 +27,35 @@
     return scale * up - scale * scale * scale * dot_sum * raw
 
 
+def inner_size(chips):
+    size = 1
+    while (2 * size) * (2 * size) <= chips and chips % (2 * size) == 0:
+        size *= 2
+    return size
+
+
 def kernel(
-    n, q_ref, p_ref, neg_ref, pairs_ref,
+    n, q_hbm, p_hbm, neg_ref, pairs_hbm,
     loss_ref, gq_ref, gp_ref, gn_ref,
-    qbuf, qfull, nraw, unit, nscale, counts, scores, expt, weights, ubuf, sibrecv, crecv, gnbuf,
+    q_ref, p_ref, pairs_ref, qbuf, qfull, nraw, unit, nscale, counts, scores, expt, weights, ubuf, sibrecv, crecv, gnbuf,
     zsend, zsib, zbuf, acc,
-    nsem, gsem, qs, qr, fs, fr, us, ur, cs, cr, zs, zr, zxs, zxr,
+    nsem, insem, gsem, qs, ys, qr, fs, fr, us, ur, cs, cr, zs, zr, zxs, zxr,
 ):
     qd, width = q_ref.shape
     half = width // 2
     pool = neg_ref.shape[0]
-    npairs = pairs_ref.shape[0]
+    npairs = pairs_ref.shape[1]
     nq = n * qd
     nc = n // 2
+    inner = inner_size(nc)
+    outer = nc // inner
     me = lax.axis_index("dp")
     chip = me // 2
     core = me - 2 * chip
     sib = me + 1 - 2 * core
+
+    a = chip // inner
+    b = chip - a * inner
 
     def ahead(k):
         return lax.rem(chip + k, nc)
@@ -57,7 +69,13 @@
             device_id={"dp": target}, device_id_type=pl.DeviceIdType.MESH,
         )
 
+    first = pltpu.make_async_copy(q_hbm, q_ref, insem.at[0])
+    second = pltpu.make_async_copy(pairs_hbm, pairs_ref, insem.at[1])
+    third = pltpu.make_async_copy(p_hbm, p_ref, insem.at[2])
     load = pltpu.make_async_copy(neg_ref, nraw, nsem)
+    first.start()
+    second.start()
+    third.start()
     load.start()
     barrier = pltpu.get_barrier_semaphore()
     pl.semaphore_signal(barrier, inc=1, device_id={"dp": sib}, device_id_type=pl.DeviceIdType.MESH)
@@ -69,34 +87,107 @@
             device_id_type=pl.DeviceIdType.MESH,
         )
 
+    first.wait()
     qx = q_ref[...].astype(f32)
     qscale = lax.rsqrt(jnp.sum(qx * qx, axis=1, keepdims=True) + norm_eps)
     qu = qx * qscale
     qbuf[me, :, :half] = jnp.concatenate([qu[:, :half], qu[:, half:]], axis=0).astype(bf16)
-    pv = pairs_ref[...].astype(f32)
-    diag = lax.broadcasted_iota(jnp.int32, (npairs, EXTRA), 0) == lax.broadcasted_iota(
-        jnp.int32, (npairs, EXTRA), 1
+    second.wait()
+    pv = jnp.concatenate(
+        [pairs_ref[...].astype(f32), jnp.full((2, EXTRA - npairs), -1.0, f32)], axis=1
     )
-    prow = jnp.sum(jnp.where(diag, pv[:, 0:1], 0.0), axis=0, keepdims=True)
-    trow = jnp.sum(jnp.where(diag, pv[:, 1:2], 0.0), axis=0, keepdims=True)
+    prow, trow = pv[0:1], pv[1:2]
     owner = jnp.floor((trow + 0.5) * (1.0 / pool))
     local_row = trow - owner * pool
-    owner = jnp.where(lax.broadcasted_iota(jnp.int32, (1, EXTRA), 1) < npairs, owner, -1.0)
     rid = lax.broadcasted_iota(jnp.int32, (16, EXTRA), 0)
     meta = jnp.where(rid == 0, prow, jnp.where(rid == 1, owner, local_row))
     qbuf[me, :, half:] = meta.astype(bf16)
 
     pl.semaphore_wait(barrier, nc)
 
-    def q_copy(k, target):
-        return remote(qbuf.at[me], qbuf.at[me], qs.at[k], qr.at[k], target)
-
-    @pl.loop(1, nc)
-    def _(k):
-        q_copy(k, 2 * ahead(k) + core).start()
-
-    q_copy(0, sib).start()
-
+    def hop(o, way):
+        slot = qbuf.at[2 * o + core]
+        target = 2 * (chip + (inner if way == 0 else -inner)) + core
+        return remote(slot, slot, qs.at[o, way], qr.at[o], target)
+
+    def across(o, shift):
+        slot = qbuf.at[2 * o + core]
+        target = 2 * (a * inner + lax.rem(b + shift, inner)) + core
+        return remote(slot, slot, ys.at[o, shift], qr.at[o], target)
+
+    def hand(o, c):
+        slot = qbuf.at[2 * o + c]
+        return remote(slot, slot, fs.at[o], fr.at[o], sib)
+
+    def arrived(o):
+        slot = qbuf.at[2 * o + core]
+        remote(slot, slot, qs.at[o, 0], qr.at[o], sib).wait_recv()
+
+    def relay(dist, act):
+        def column(o, up, down):
+            if up is not None:
+                @pl.when(up)
+                def _():
+                    act(hop(o, 0))
+            if down is not None:
+                @pl.when(down)
+                def _():
+                    act(hop(o, 1))
+
+            @pl.loop(1, inner)
+            def _(shift):
+                act(across(o, shift))
+
+            act(hand(o, core))
+
+        if dist == 0:
+            column(chip, a + 1 < outer, a > 0)
+            return
+
+        @pl.when(a >= dist)
+        def _():
+            o = chip - dist * inner
+            if act is launch:
+                arrived(o)
+            column(o, a + 1 < outer, None)
+
+        @pl.when(a + dist < outer)
+        def _():
+            o = chip + dist * inner
+            if act is launch:
+                arrived(o)
+            column(o, None, a > 0)
+
+    def relay_side(dist, act):
+        def row(line):
+            @pl.loop(1, inner)
+            def _(shift):
+                o = line * inner + lax.rem(b + inner - shift, inner)
+                if act is launch:
+                    arrived(o)
+                act(hand(o, core))
+
+        if dist == 0:
+            row(a)
+            return
+
+        @pl.when(a >= dist)
+        def _():
+            row(a - dist)
+
+        @pl.when(a + dist < outer)
+        def _():
+            row(a + dist)
+
+    def launch(copy):
+        copy.start()
+
+    def sent(copy):
+        copy.wait_send()
+
+    relay(0, launch)
+
+    third.wait()
     px = p_ref[...].astype(f32)
     pscale = lax.rsqrt(jnp.sum(px * px, axis=1, keepdims=True) + norm_eps)
     unit[pool : pool + 16, :] = jnp.concatenate(
@@ -105,38 +196,37 @@
     unit[pool + 16 :, :] = jnp.zeros((unit.shape[0] - pool - 16, width), bf16)
     load.wait()
 
-    @pl.loop(0, pool // 16)
-    def _(b):
-        rows = pl.ds(pl.multiple_of(b * 16, 16), 16)
-        x = nraw[rows, :].astype(f32)
-        s = lax.rsqrt(jnp.sum(x * x, axis=1, keepdims=True) + norm_eps)
-        nscale[rows, :] = s
-        unit[rows, :] = (x * s).astype(bf16)
-
-    def f_copy(k, c):
-        slot = 2 * behind(k) + c
-        return remote(qbuf.at[slot], qbuf.at[slot], fs.at[k], fr.at[k], sib)
-
-    @pl.loop(1, nc)
-    def _(k):
-        slot = 2 * behind(k) + core
-        remote(qbuf.at[slot], qbuf.at[slot], qs.at[k], qr.at[k], sib).wait_recv()
-        f_copy(k, core).start()
+    def normalise(lo, hi):
+        @pl.loop(lo, hi)
+        def _(blk):
+            rows = pl.ds(pl.multiple_of(blk * 16, 16), 16)
+            x = nraw[rows, :].astype(f32)
+            s = lax.rsqrt(jnp.sum(x * x, axis=1, keepdims=True) + norm_eps)
+            nscale[rows, :] = s
+            unit[rows, :] = (x * s).astype(bf16)
+
+    blocks = pool // 16
+    normalise(0, blocks // outer)
+    for dist in range(1, outer):
+        relay(dist, launch)
+        relay_side(dist - 1, launch)
+        normalise(blocks * dist // outer, blocks * (dist + 1) // outer)
+    relay_side(outer - 1, launch)
 
     arow = lax.broadcasted_iota(jnp.int32, (unit.shape[0], nq), 0)
     counts[...] = jnp.where((arow >= pool) & (arow < pool + qd), 1.0, 0.0)
     mef = me.astype(f32)
 
     def place(j):
-        a = qbuf[2 * j].astype(f32)
-        b = qbuf[2 * j + 1].astype(f32)
+        left = qbuf[2 * j].astype(f32)
+        right = qbuf[2 * j + 1].astype(f32)
         rows = pl.ds(pl.multiple_of(j * 16, 16), 16)
-        qfull[rows, :half] = jnp.concatenate([a[:8, :half], b[:8, :half]], axis=0).astype(bf16)
-        qfull[rows, half:] = jnp.concatenate([a[8:, :half], b[8:, :half]], axis=0).astype(bf16)
+        qfull[rows, :half] = jnp.concatenate([left[:8, :half], right[:8, :half]], axis=0).astype(bf16)
+        qfull[rows, half:] = jnp.concatenate([left[8:, :half], right[8:, :half]], axis=0).astype(bf16)
         pool_id = lax.broadcasted_iota(jnp.int32, (pool, EXTRA), 0).astype(f32)
         query_id = lax.broadcasted_iota(jnp.int32, (nq, EXTRA), 0).astype(f32)
         hot_t, hot_q = [], []
-        for part, c in ((a, 0), (b, 1)):
+        for part, c in ((left, 0), (right, 1)):
             m = part[:8, half:]
             want = jnp.where(m[1:2] == mef, m[2:3], -1.0)
             ask = m[0:1] + ((2 * j + c) * qd).astype(f32)
@@ -146,12 +236,12 @@
             jnp.concatenate(hot_t, axis=1), jnp.concatenate(hot_q, axis=1)
         )
 
-    remote(qbuf.at[sib], qbuf.at[sib], qs.at[0], qr.at[0], sib).wait_recv()
+    hand(chip, 1 - core).wait_recv()
     place(chip)
 
     @pl.loop(1, nc)
     def _(k):
-        f_copy(k, 1 - core).wait_recv()
+        hand(behind(k), 1 - core).wait_recv()
         place(behind(k))
 
     zero = jnp.zeros((1, 128), f32)
@@ -268,17 +358,18 @@
     qg = inv_temp * (own_g + rest * jnp.exp(-log_own))
     gq_ref[...] = norm_grad(qx, qscale, qg)
 
-    q_copy(0, sib).wait_send()
     z_sib.wait_send()
     u_copy(0, chip).wait_send()
 
     @pl.loop(1, nc)
     def _(k):
-        q_copy(k, sib).wait_send()
-        f_copy(k, core).wait_send()
         z_copy(k, chip).wait_send()
         u_copy(k, ahead(k)).wait_send()
         c_copy(k, ahead(k)).wait_send()
+
+    for dist in range(outer):
+        relay(dist, sent)
+        relay_side(dist, sent)
 
     save.wait()
 
@@ -292,7 +383,7 @@
     half = width // 2
     rows = pool + 128
     vm = pl.BlockSpec(memory_space=pltpu.VMEM)
-    anys = pl.BlockSpec(memory_space=pl.ANY)
+    hbm = pl.BlockSpec(memory_space=pltpu.HBM)
     dma = pltpu.SemaphoreType.DMA
     loss, gq, gp, gn = pl.pallas_call(
         functools.partial(kernel, n),
@@ -302,9 +393,12 @@
             jax.ShapeDtypeStruct((qd, width), f32),
             jax.ShapeDtypeStruct((pool, width), bf16),
         ),
-        in_specs=[vm, vm, anys, vm],
-        out_specs=(vm, vm, vm, anys),
+        in_specs=[hbm, hbm, hbm, hbm],
+        out_specs=(vm, vm, vm, hbm),
         scratch_shapes=[
+            pltpu.VMEM((qd, width), bf16),
+            pltpu.VMEM((qd, width), bf16),
+            pltpu.VMEM((2, pairs.shape[0]), jnp.int32),
             pltpu.VMEM((n, 16, half + EXTRA), bf16),
             pltpu.VMEM((nq, width), bf16),
             pltpu.VMEM((pool, width), bf16),
@@ -322,15 +416,16 @@
             pltpu.VMEM((8, nq), f32),
             pltpu.VMEM((nc, 8, nq), f32),
             pltpu.VMEM((16, half), f32),
-            dma, dma,
-            dma((nc,)), dma((nc,)), dma((nc,)), dma((nc,)), dma((nc,)), dma((nc,)),
+            dma, dma((3,)), dma,
+            dma((nc, 2)), dma((nc, inner_size(nc))), dma((nc,)), dma((nc,)), dma((nc,)),
+            dma((nc,)), dma((nc,)),
             dma((nc,)), dma((nc,)), dma((1,)), dma((1,)), dma((nc,)), dma((nc,)),
         ],
         compiler_params=pltpu.CompilerParams(
             collective_id=0, has_side_effects=True,
-            vmem_limit_bytes=(56 if n > 32 else 40) * 1024 * 1024,
+            vmem_limit_bytes=58 * 1024 * 1024,
         ),
-    )(queries, passages, negatives, pairs)
+    )(queries, passages, negatives, pairs.T)
     return loss.reshape(qd), gq, gp, gn.astype(f32)
 
 

time: 45.5 us -> 43.3 us (0.952)
  the two profiles are of different devices: /device:TPU:29 before, /device:TPU:13 now
where the time goes in v2:
time: 43.3 us; the launch traced here: 43 us
  Pallas kernels  35.6 us (82%)
  other arithmetic  5.44 us (13%)
  local copies, waits for them, and re-layouts  1.32 us (3%)
  between operations  0.64 us (1%)
    pallas_call x1, Pallas kernels, local(): pl.pallas_call(functools.partial(kernel, n), out_shape=(jax.ShapeDtypeStr...  35.6 us
    convert_element_type x1, other arithmetic, local(): return (loss.reshape(qd), gq, gp, gn.astype(f32))  4.14 us
    unnamed x6, local copies, waits for them, and re-layouts  1.32 us
    pallas_call x1, other arithmetic, local(): pl.pallas_call(functools.partial(kernel, n), out_shape=(jax.ShapeDtypeStr...  1.3 us

profile of v2, /device:TPU:13, one launch (start us, length us, event | category | flops | bytes accessed | tf_op | source)
XLA Modules:
  0.0 43.0 jit_solution(4186137972963898575)
XLA Ops:
  0.6 35.6 %shard_map.75 = (f32[8,1]{1,0:T(8,128)}, f32[8,4096]{1,0:T(8,128)}, f32[8,4096]{1,0:T(8,128)}, bf16[256,4096]{1,0:T(8,128)(2,1)}) custom-call(bf16[8,4096]{1,0:T(8,128)(2,1)} %q_hbm.1, bf16[8,4096]{1,0:T(8,128)(2,1)} %p_hbm.1, bf16[256,4096]{1,0:T(8,128)(2,1)} %neg_ref.1, s32[2,112]{1,0:T(2,128)} %bitcast.1), custom_call_target="tpu_custom_call" | custom-call | tf_op jit(solution)/shard_map/pallas_call | solution.py:388
  36.3 1.3 %reduce = f32[8]{0:T(128)} reduce(f32[8,1]{1,0:T(8,128)} %get-tuple-element.8, f32[]{:T(128)} %constant.3), dimensions={1}, to_apply=%get-tuple-element.8.reduce_sub_computation | reduce | bytes 68 | tf_op jit(solution)/shard_map/pallas_call | solution.py:388
  37.6 0.0 copy-start.1
  37.6 0.0 copy-start
  37.6 4.1 %convert_element_type.3 = f32[256,4096]{1,0:T(8,128)} convert(bf16[256,4096]{1,0:T(8,128)(2,1)} %get-tuple-element.11) | non-fusion elementwise | flops 1048576 | bytes 6291456 | tf_op jit(solution)/shard_map/convert_element_type | solution.py:429
  41.7 0.0 copy-done.1
  41.7 0.7 %copy.10 = f32[8,4096]{1,0:T(8,128)} copy(f32[8,4096]{1,0:T(8,128)S(1)} %copy-done.1) | data formatting | bytes 262144
  42.4 0.0 copy-done
  42.4 0.7 %copy.11 = f32[8,4096]{1,0:T(8,128)} copy(f32[8,4096]{1,0:T(8,128)S(1)} %copy-done) | data formatting | bytes 262144
Async XLA Ops:
  37.6 4.1 %copy-start.1 = (f32[8,4096]{1,0:T(8,128)S(1)}, f32[8,4096]{1,0:T(8,128)}, u32[]{:S(2)}) copy-start(f32[8,4096]{1,0:T(8,128)} %get-tuple-element.17) | copy-start | bytes 393220
  37.6 4.8 %copy-start = (f32[8,4096]{1,0:T(8,128)S(1)}, f32[8,4096]{1,0:T(8,128)}, u32[]{:S(2)}) copy-start(f32[8,4096]{1,0:T(8,128)} %get-tuple-element.18) | copy-start | bytes 393220

commit v3 on v2

--- a/solution.py
+++ b/solution.py
@@ -105,10 +105,10 @@
 
     pl.semaphore_wait(barrier, nc)
 
-    def hop(o, way):
-        slot = qbuf.at[2 * o + core]
-        target = 2 * (chip + (inner if way == 0 else -inner)) + core
-        return remote(slot, slot, qs.at[o, way], qr.at[o], target)
+    def along(shift):
+        slot = qbuf.at[me]
+        target = 2 * (lax.rem(a + shift, outer) * inner + b) + core
+        return remote(slot, slot, qs.at[shift], qr.at[chip], target)
 
     def across(o, shift):
         slot = qbuf.at[2 * o + core]
@@ -121,71 +121,33 @@
 
     def arrived(o):
         slot = qbuf.at[2 * o + core]
-        remote(slot, slot, qs.at[o, 0], qr.at[o], sib).wait_recv()
-
-    def relay(dist, act):
-        def column(o, up, down):
-            if up is not None:
-                @pl.when(up)
-                def _():
-                    act(hop(o, 0))
-            if down is not None:
-                @pl.when(down)
-                def _():
-                    act(hop(o, 1))
-
-            @pl.loop(1, inner)
-            def _(shift):
-                act(across(o, shift))
-
-            act(hand(o, core))
-
-        if dist == 0:
-            column(chip, a + 1 < outer, a > 0)
-            return
-
-        @pl.when(a >= dist)
-        def _():
-            o = chip - dist * inner
-            if act is launch:
-                arrived(o)
-            column(o, a + 1 < outer, None)
-
-        @pl.when(a + dist < outer)
-        def _():
-            o = chip + dist * inner
-            if act is launch:
-                arrived(o)
-            column(o, None, a > 0)
-
-    def relay_side(dist, act):
-        def row(line):
-            @pl.loop(1, inner)
-            def _(shift):
-                o = line * inner + lax.rem(b + inner - shift, inner)
-                if act is launch:
-                    arrived(o)
-                act(hand(o, core))
-
-        if dist == 0:
-            row(a)
-            return
-
-        @pl.when(a >= dist)
-        def _():
-            row(a - dist)
-
-        @pl.when(a + dist < outer)
-        def _():
-            row(a + dist)
-
-    def launch(copy):
-        copy.start()
-
-    def sent(copy):
-        copy.wait_send()
-
-    relay(0, launch)
+        remote(slot, slot, qs.at[0], qr.at[o], sib).wait_recv()
+
+    def line(shift):
+        return lax.rem(a + outer - shift, outer)
+
+    def spread(o):
+        @pl.loop(1, inner)
+        def _(shift):
+            across(o, shift).start()
+
+        hand(o, core).start()
+
+    def side(shift, act):
+        @pl.loop(1, inner)
+        def _(turn):
+            act(line(shift) * inner + lax.rem(b + inner - turn, inner))
+
+    def pass_on(o):
+        arrived(o)
+        hand(o, core).start()
+
+    def passed(o):
+        hand(o, core).wait_send()
+
+    for shift in range(1, outer):
+        along(shift).start()
+    spread(chip)
 
     third.wait()
     px = p_ref[...].astype(f32)
@@ -207,11 +169,13 @@
 
     blocks = pool // 16
     normalise(0, blocks // outer)
-    for dist in range(1, outer):
-        relay(dist, launch)
-        relay_side(dist - 1, launch)
-        normalise(blocks * dist // outer, blocks * (dist + 1) // outer)
-    relay_side(outer - 1, launch)
+    for shift in range(1, outer):
+        o = line(shift) * inner + b
+        arrived(o)
+        spread(o)
+        side(shift - 1, pass_on)
+        normalise(blocks * shift // outer, blocks * (shift + 1) // outer)
+    side(outer - 1, pass_on)
 
     arow = lax.broadcasted_iota(jnp.int32, (unit.shape[0], nq), 0)
     counts[...] = jnp.where((arow >= pool) & (arow < pool + qd), 1.0, 0.0)
@@ -314,7 +278,9 @@
     self_score = jnp.sum(
         jnp.where(own, scores[pool : pool + 8, :], 0.0), axis=1, keepdims=True
     )
-    loss_ref[...] = log_own - self_score
+    loss_ref[...] = jnp.sum(
+        jnp.where(lane_q == row_q, log_own - self_score, 0.0), axis=0, keepdims=True
+    )[:, :128]
     positive = (arow >= pool) & (
         arow - pool + me * qd == lax.broadcasted_iota(jnp.int32, arow.shape, 1)
     ) & (arow < pool + qd)
@@ -367,11 +333,26 @@
         u_copy(k, ahead(k)).wait_send()
         c_copy(k, ahead(k)).wait_send()
 
-    for dist in range(outer):
-        relay(dist, sent)
-        relay_side(dist, sent)
+    for shift in range(outer):
+        if shift:
+            along(shift).wait_send()
+        o = line(shift) * inner + b
+        for turn in range(1, inner):
+            across(o, turn).wait_send()
+        hand(o, core).wait_send()
+        side(shift, passed)
 
     save.wait()
+
+
+def finish(loss_ref, gq_ref, gp_ref, gn_ref, loss_out, gq_out, gp_out, gn_out):
+    @pl.when(pl.program_id(0) == 0)
+    def _():
+        loss_out[...] = loss_ref[0, : loss_out.shape[0]]
+        gq_out[...] = gq_ref[...]
+        gp_out[...] = gp_ref[...]
+
+    gn_out[...] = gn_ref[...].astype(f32)
 
 
 def local(queries, passages, negatives, pairs):
@@ -388,7 +369,7 @@
     loss, gq, gp, gn = pl.pallas_call(
         functools.partial(kernel, n),
         out_shape=(
-            jax.ShapeDtypeStruct((qd, 1), f32),
+            jax.ShapeDtypeStruct((1, 128), f32),
             jax.ShapeDtypeStruct((qd, width), f32),
             jax.ShapeDtypeStruct((qd, width), f32),
             jax.ShapeDtypeStruct((pool, width), bf16),
@@ -417,7 +398,7 @@
             pltpu.VMEM((nc, 8, nq), f32),
             pltpu.VMEM((16, half), f32),
             dma, dma((3,)), dma,
-            dma((nc, 2)), dma((nc, inner_size(nc))), dma((nc,)), dma((nc,)), dma((nc,)),
+            dma((nc // inner_size(nc),)), dma((nc, inner_size(nc))), dma((nc,)), dma((nc,)), dma((nc,)),
             dma((nc,)), dma((nc,)),
             dma((nc,)), dma((nc,)), dma((1,)), dma((1,)), dma((nc,)), dma((nc,)),
         ],
@@ -426,7 +407,22 @@
             vmem_limit_bytes=58 * 1024 * 1024,
         ),
     )(queries, passages, negatives, pairs.T)
-    return loss.reshape(qd), gq, gp, gn.astype(f32)
+    block = 64
+    whole = pl.BlockSpec((qd, width), lambda i: (0, 0))
+    piece = pl.BlockSpec((block, width), lambda i: (i, 0))
+    return pl.pallas_call(
+        finish,
+        grid=(pool // block,),
+        out_shape=(
+            jax.ShapeDtypeStruct((qd,), f32),
+            jax.ShapeDtypeStruct((qd, width), f32),
+            jax.ShapeDtypeStruct((qd, width), f32),
+            jax.ShapeDtypeStruct((pool, width), f32),
+        ),
+        in_specs=[pl.BlockSpec((1, 128), lambda i: (0, 0)), whole, whole, piece],
+        out_specs=(pl.BlockSpec((qd,), lambda i: (0,)), whole, whole, piece),
+        compiler_params=pltpu.CompilerParams(vmem_limit_bytes=60 * 1024 * 1024),
+    )(loss, gq, gp, gn)
 
 
 def solution(mesh):

time: 43.3 us -> 41.8 us (0.965)
  other arithmetic: 5.44 us -> 0 us
  Pallas kernels: 35.6 us -> 41 us
  local copies, waits for them, and re-layouts: 1.32 us -> 0 us
    pallas_call x0 -> x1, Pallas kernels: none -> 4.33 us  [local(): pl.pallas_call(finish, grid=(pool // block,), out_shape=(jax.ShapeDtypeSt...]
    convert_element_type x1 -> x0, other arithmetic: 4.14 us -> none  [local(): return (loss.reshape(qd), gq, gp, gn.astype(f32))]
    unnamed x6 -> x0, local copies, waits for them, and re-layouts: 1.32 us -> none
    pallas_call x1 -> x0, other arithmetic: 1.3 us -> none  [local(): pl.pallas_call(functools.partial(kernel, n), out_shape=(jax.ShapeDtypeStr...]
    pallas_call x1, Pallas kernels: 35.6 us -> 36.7 us  [local(): pl.pallas_call(functools.partial(kernel, n), out_shape=(jax.ShapeDtypeStr...]
where the time goes in v3:
time: 41.8 us; the launch traced here: 41.6 us
  Pallas kernels  41 us (98%)
  between operations  0.64 us (2%)
    pallas_call x1, Pallas kernels, local(): pl.pallas_call(functools.partial(kernel, n), out_shape=(jax.ShapeDtypeStr...  36.7 us
    pallas_call x1, Pallas kernels, local(): pl.pallas_call(finish, grid=(pool // block,), out_shape=(jax.ShapeDtypeSt...  4.33 us

profile of v3, /device:TPU:13, one launch (start us, length us, event | category | flops | bytes accessed | tf_op | source)
XLA Modules:
  0.0 41.6 jit_solution(15230450999148171853)
XLA Ops:
  0.6 36.7 %shard_map.75 = (f32[1,128]{1,0:T(1,128)}, f32[8,4096]{1,0:T(8,128)}, f32[8,4096]{1,0:T(8,128)}, bf16[256,4096]{1,0:T(8,128)(2,1)}) custom-call(bf16[8,4096]{1,0:T(8,128)(2,1)} %q_hbm.1, bf16[8,4096]{1,0:T(8,128)(2,1)} %p_hbm.1, bf16[256,4096]{1,0:T(8,128)(2,1)} %neg_ref.1, s32[2,112]{1,0:T(2,128)} %bitcast.1), custom_call_target="tpu_custom_call" | custom-call | tf_op jit(solution)/shard_map/pallas_call | solution.py:369
  37.3 4.3 %shard_map.76 = (f32[8]{0:T(128)}, f32[8,4096]{1,0:T(8,128)}, f32[8,4096]{1,0:T(8,128)}, f32[256,4096]{1,0:T(8,128)}) custom-call(f32[1,128]{1,0:T(1,128)} %get-tuple-element.8.loss_ref, f32[8,4096]{1,0:T(8,128)} %get-tuple-element.9.gq_ref, f32[8,4096]{1,0:T(8,128)} %get-tuple-element.10.gp_ref, bf16[256,4096]{1,0:T(8,128)(2,1)} %get-tuple-element.11.gn_ref), custom_call_target="tpu_custom_call" | custom-call | tf_op jit(solution)/shard_map/pallas_call | solution.py:413

commit v4 on v3

--- a/solution.py
+++ b/solution.py
@@ -345,14 +345,36 @@
     save.wait()
 
 
-def finish(loss_ref, gq_ref, gp_ref, gn_ref, loss_out, gq_out, gp_out, gn_out):
-    @pl.when(pl.program_id(0) == 0)
-    def _():
-        loss_out[...] = loss_ref[0, : loss_out.shape[0]]
-        gq_out[...] = gq_ref[...]
-        gp_out[...] = gp_ref[...]
-
-    gn_out[...] = gn_ref[...].astype(f32)
+def finish(
+    loss_ref, gq_ref, gp_ref, gn_ref, loss_out, gq_out, gp_out, gn_out,
+    narrow, full, in_sem, out_sem, q_sem, p_sem,
+):
+    parts = 8
+    block = narrow.shape[0] // parts
+    rows = [pl.ds(i * block, block) for i in range(parts)]
+    reads = [
+        pltpu.make_async_copy(gn_ref.at[r], narrow.at[r], in_sem.at[i])
+        for i, r in enumerate(rows)
+    ]
+    writes = [
+        pltpu.make_async_copy(full.at[r], gn_out.at[r], out_sem.at[i])
+        for i, r in enumerate(rows)
+    ]
+    q_copy = pltpu.make_async_copy(gq_ref, gq_out, q_sem)
+    p_copy = pltpu.make_async_copy(gp_ref, gp_out, p_sem)
+    for read in reads:
+        read.start()
+    q_copy.start()
+    p_copy.start()
+    loss_out[...] = loss_ref[0, : loss_out.shape[0]]
+    for i, r in enumerate(rows):
+        reads[i].wait()
+        full[r, :] = narrow[r, :].astype(f32)
+        writes[i].start()
+    for write in writes:
+        write.wait()
+    q_copy.wait()
+    p_copy.wait()
 
 
 def local(queries, passages, negatives, pairs):
@@ -407,20 +429,20 @@
             vmem_limit_bytes=58 * 1024 * 1024,
         ),
     )(queries, passages, negatives, pairs.T)
-    block = 64
-    whole = pl.BlockSpec((qd, width), lambda i: (0, 0))
-    piece = pl.BlockSpec((block, width), lambda i: (i, 0))
     return pl.pallas_call(
         finish,
-        grid=(pool // block,),
         out_shape=(
             jax.ShapeDtypeStruct((qd,), f32),
             jax.ShapeDtypeStruct((qd, width), f32),
             jax.ShapeDtypeStruct((qd, width), f32),
             jax.ShapeDtypeStruct((pool, width), f32),
         ),
-        in_specs=[pl.BlockSpec((1, 128), lambda i: (0, 0)), whole, whole, piece],
-        out_specs=(pl.BlockSpec((qd,), lambda i: (0,)), whole, whole, piece),
+        in_specs=[vm, hbm, hbm, hbm],
+        out_specs=(vm, hbm, hbm, hbm),
+        scratch_shapes=[
+            pltpu.VMEM((pool, width), bf16), pltpu.VMEM((pool, width), f32),
+            dma((8,)), dma((8,)), dma, dma,
+        ],
         compiler_params=pltpu.CompilerParams(vmem_limit_bytes=60 * 1024 * 1024),
     )(loss, gq, gp, gn)
 

time: 41.8 us -> 47.8 us (1.14)
  Pallas kernels: 41 us -> 47 us
    pallas_call x1, Pallas kernels: 4.33 us -> 10.3 us  [local(): pl.pallas_call(finish, out_shape=(jax.ShapeDtypeStruct((qd,), f32), jax.S...]
where the time goes in v4:
time: 47.8 us; the launch traced here: 47.6 us
  Pallas kernels  47 us (98%)
  between operations  0.64 us (1%)
    pallas_call x1, Pallas kernels, local(): pl.pallas_call(functools.partial(kernel, n), out_shape=(jax.ShapeDtypeStr...  36.7 us
    pallas_call x1, Pallas kernels, local(): pl.pallas_call(finish, out_shape=(jax.ShapeDtypeStruct((qd,), f32), jax.S...  10.3 us

profile of v4, /device:TPU:13, one launch (start us, length us, event | category | flops | bytes accessed | tf_op | source)
XLA Modules:
  0.0 47.6 jit_solution(12696333002106835512)
XLA Ops:
  0.6 36.7 %shard_map.75 = (f32[1,128]{1,0:T(1,128)}, f32[8,4096]{1,0:T(8,128)}, f32[8,4096]{1,0:T(8,128)}, bf16[256,4096]{1,0:T(8,128)(2,1)}) custom-call(bf16[8,4096]{1,0:T(8,128)(2,1)} %q_hbm.1, bf16[8,4096]{1,0:T(8,128)(2,1)} %p_hbm.1, bf16[256,4096]{1,0:T(8,128)(2,1)} %neg_ref.1, s32[2,112]{1,0:T(2,128)} %bitcast.1), custom_call_target="tpu_custom_call" | custom-call | tf_op jit(solution)/shard_map/pallas_call | solution.py:391
  37.3 10.3 %shard_map.76 = (f32[8]{0:T(128)}, f32[8,4096]{1,0:T(8,128)}, f32[8,4096]{1,0:T(8,128)}, f32[256,4096]{1,0:T(8,128)}) custom-call(f32[1,128]{1,0:T(1,128)} %get-tuple-element.8.loss_ref, f32[8,4096]{1,0:T(8,128)} %get-tuple-element.9.gq_ref, f32[8,4096]{1,0:T(8,128)} %get-tuple-element.10.gp_ref, bf16[256,4096]{1,0:T(8,128)(2,1)} %get-tuple-element.11.gn_ref), custom_call_target="tpu_custom_call" | custom-call | tf_op jit(solution)/shard_map/pallas_call | solution.py:432

commit v5 on v4

--- a/solution.py
+++ b/solution.py
@@ -347,7 +347,7 @@
 
 def finish(
     loss_ref, gq_ref, gp_ref, gn_ref, loss_out, gq_out, gp_out, gn_out,
-    narrow, full, in_sem, out_sem, q_sem, p_sem,
+    narrow, full, in_sem, out_sem,
 ):
     parts = 8
     block = narrow.shape[0] // parts
@@ -360,12 +360,10 @@
         pltpu.make_async_copy(full.at[r], gn_out.at[r], out_sem.at[i])
         for i, r in enumerate(rows)
     ]
-    q_copy = pltpu.make_async_copy(gq_ref, gq_out, q_sem)
-    p_copy = pltpu.make_async_copy(gp_ref, gp_out, p_sem)
     for read in reads:
         read.start()
-    q_copy.start()
-    p_copy.start()
+    gq_out[...] = gq_ref[...]
+    gp_out[...] = gp_ref[...]
     loss_out[...] = loss_ref[0, : loss_out.shape[0]]
     for i, r in enumerate(rows):
         reads[i].wait()
@@ -373,8 +371,6 @@
         writes[i].start()
     for write in writes:
         write.wait()
-    q_copy.wait()
-    p_copy.wait()
 
 
 def local(queries, passages, negatives, pairs):
@@ -437,11 +433,11 @@
             jax.ShapeDtypeStruct((qd, width), f32),
             jax.ShapeDtypeStruct((pool, width), f32),
         ),
-        in_specs=[vm, hbm, hbm, hbm],
-        out_specs=(vm, hbm, hbm, hbm),
+        in_specs=[vm, vm, vm, hbm],
+        out_specs=(vm, vm, vm, hbm),
         scratch_shapes=[
             pltpu.VMEM((pool, width), bf16), pltpu.VMEM((pool, width), f32),
-            dma((8,)), dma((8,)), dma, dma,
+            dma((8,)), dma((8,)),
         ],
         compiler_params=pltpu.CompilerParams(vmem_limit_bytes=60 * 1024 * 1024),
     )(loss, gq, gp, gn)

time: 47.8 us -> 42.3 us (0.88)
  Pallas kernels: 47 us -> 41.5 us
    pallas_call x1, Pallas kernels: 10.3 us -> 4.8 us  [local(): pl.pallas_call(finish, out_shape=(jax.ShapeDtypeStruct((qd,), f32), jax.S...]
where the time goes in v5:
time: 42.3 us; the launch traced here: 42.1 us
  Pallas kernels  41.5 us (98%)
  between operations  0.64 us (2%)
    pallas_call x1, Pallas kernels, local(): pl.pallas_call(functools.partial(kernel, n), out_shape=(jax.ShapeDtypeStr...  36.7 us
    pallas_call x1, Pallas kernels, local(): pl.pallas_call(finish, out_shape=(jax.ShapeDtypeStruct((qd,), f32), jax.S...  4.8 us

profile of v5, /device:TPU:13, one launch (start us, length us, event | category | flops | bytes accessed | tf_op | source)
XLA Modules:
  0.0 42.1 jit_solution(10854538623168276797)
XLA Ops:
  0.6 36.7 %shard_map.75 = (f32[1,128]{1,0:T(1,128)}, f32[8,4096]{1,0:T(8,128)}, f32[8,4096]{1,0:T(8,128)}, bf16[256,4096]{1,0:T(8,128)(2,1)}) custom-call(bf16[8,4096]{1,0:T(8,128)(2,1)} %q_hbm.1, bf16[8,4096]{1,0:T(8,128)(2,1)} %p_hbm.1, bf16[256,4096]{1,0:T(8,128)(2,1)} %neg_ref.1, s32[2,112]{1,0:T(2,128)} %bitcast.1), custom_call_target="tpu_custom_call" | custom-call | tf_op jit(solution)/shard_map/pallas_call | solution.py:387
  37.3 4.8 %shard_map.76 = (f32[8]{0:T(128)}, f32[8,4096]{1,0:T(8,128)}, f32[8,4096]{1,0:T(8,128)}, f32[256,4096]{1,0:T(8,128)}) custom-call(f32[1,128]{1,0:T(1,128)} %get-tuple-element.8.loss_ref, f32[8,4096]{1,0:T(8,128)} %get-tuple-element.9.gq_ref, f32[8,4096]{1,0:T(8,128)} %get-tuple-element.10.gp_ref, bf16[256,4096]{1,0:T(8,128)(2,1)} %get-tuple-element.11.gn_ref), custom_call_target="tpu_custom_call" | custom-call | tf_op jit(solution)/shard_map/pallas_call | solution.py:428
